TPU v7x, 32 devices: a whole 2x2x4 slice. The times are simulated.
32 devices in a mesh: groups: 2 (over x), dp: 8 (over z, y), tensor: 2 (over core).
Axes of the slice: x: 2, y: 2, z: 4, core: 2. Of those that a mesh axis runs over, the one named last changes fastest.
Arguments:
- queries: bfloat16 [2048, 8192], P(('groups', 'dp'), 'tensor'), parts along dimension 0
- response_key_rows: bfloat16 [2048, 1024], P(('groups', 'dp'), 'tensor'), parts along dimension 0
- response_value_rows: bfloat16 [2048, 1024], P(('groups', 'dp'), 'tensor'), parts along dimension 0, may hold values from -6 to 6
- shared_prompt_keys: bfloat16 [16, 768, 1024], P(('groups', 'dp'), None, 'tensor'), parts along dimension 0, may hold values from -6 to 6
- shared_prompt_values: bfloat16 [16, 768, 1024], P(('groups', 'dp'), None, 'tensor'), parts along dimension 0, may hold values from -6 to 6
- grad_out: bfloat16 [2048, 8192], P(('groups', 'dp'), 'tensor'), parts along dimension 0, may hold values from -6 to 6
- lengths: int32 [64], P('groups'), parts along dimension 0, may hold values from 1 to 64, as said below
- packing: int32 [16, 6], P(('groups', 'dp')), parts along dimension 0, may hold values from -1 to 31, as said below
- prompt_of: int32 [64], P('groups'), parts along dimension 0, may hold values from 0 to 7, as said below
- prompt_owner: int32 [16], P('groups'), parts along dimension 0, may hold values from 0 to 7, as said below
Outputs:
- attn_out: bfloat16 [2048, 8192], P(('groups', 'dp'), 'tensor'), parts along dimension 0
- grad_queries: bfloat16 [2048, 8192], P(('groups', 'dp'), 'tensor'), parts along dimension 0
- grad_response_keys: bfloat16 [2048, 1024], P(('groups', 'dp'), 'tensor'), parts along dimension 0
- grad_response_values: bfloat16 [2048, 1024], P(('groups', 'dp'), 'tensor'), parts along dimension 0
- grad_prompt_keys: bfloat16 [16, 768, 1024], P(('groups', 'dp'), None, 'tensor'), parts along dimension 0
- grad_prompt_values: bfloat16 [16, 768, 1024], P(('groups', 'dp'), None, 'tensor'), parts along dimension 0
There are 2 independent parts, one for each index of `groups`. A program takes and returns all parts, laid end to end along the dimension named above; each array names one. Nothing has to cross between parts.
Inputs may be any that keep to these rules, and one draw needn't show every extreme that they name: `prompt_of`: each prompt has exactly 4 responses. A permutation: prompt p sits at slot prompt_owner[p] of shared_prompt_keys and shared_prompt_values. `packing`: every response is named in exactly one list. List b names responses of the prompt at slot b first, then responses of the prompt at slot (b - 1) mod 8, then -1 entries; it names at least 2 responses. `lengths`: the responses of one list have 128 tokens or fewer together; some response has 64 tokens.
All inputs are finite; a program needn't handle non-finite values.
Results may differ from a plain program's by a relative error of at most 0.0035.
The roundings to bfloat16 on the way count: a program that leaves them out, or rounds other values in their place, can miss the bound.
Values may be sent and summed in bfloat16 or wider, within the bound.
No kernel may reach another device: no remote copies, remote signals or barrier semaphores. Data moves between devices by JAX's collectives and lax.ppermute only.
A program may use at most 64 MiB of HBM per device.

v0:
```python
import functools

import jax
import jax.numpy as jnp
from jax import lax
from jax.experimental import pallas as pl
from jax.experimental.pallas import tpu as pltpu
from jax.sharding import PartitionSpec as P

HEAD_WIDTH = 128
TILE_ROWS = 32
SCORE_SCALE = HEAD_WIDTH ** -0.5
LOG2_E = 1.4426950408889634
NEGATIVE = -1e30
F32 = jnp.float32
BF16 = jnp.bfloat16
VMEM_LIMIT = 60 * 1024 * 1024
KEY_CHUNK = 256
ARRIVED_CHUNK = 768


def shifted(value, axis, steps):
    count = lax.axis_size(axis)
    pairs = [(source, (source + steps) % count) for source in range(count)]
    return lax.ppermute(value, axis, pairs)


def dot(left, right):
    return lax.dot_general(
        left, right, (((1,), (0,)), ((), ())), preferred_element_type=F32
    )


def dot_nt(left, right):
    return lax.dot_general(
        left, right, (((1,), (1,)), ((), ())), preferred_element_type=F32
    )


def chunks(length, size):
    return [slice(start, min(start + size, length)) for start in range(0, length, size)]


def plan(scalars):
    device, packing, lengths, prompt_of, prompt_owner = scalars
    own = jnp.int32(0)
    total = jnp.int32(0)
    ends = []
    for slot in range(packing.shape[1]):
        entry = packing[0, slot]
        used = entry >= 0
        index = jnp.maximum(entry, 0)
        length = jnp.where(used, lengths[index], 0)
        holder = prompt_owner[prompt_of[index]]
        own = own + jnp.where(holder == device[0], length, 0)
        total = total + length
        ends.append(total)
    return own, total, ends


def tile_of(ref, row, group, first=0):
    columns = [slice(first + g * HEAD_WIDTH, first + (g + 1) * HEAD_WIDTH) for g in range(group)]
    return jnp.concatenate([ref[pl.ds(row, TILE_ROWS), part] for part in columns], axis=0)


def put_tile(ref, row, group, value, first=0):
    for g in range(group):
        columns = slice(first + g * HEAD_WIDTH, first + (g + 1) * HEAD_WIDTH)
        ref[pl.ds(row, TILE_ROWS), columns] = value[g * TILE_ROWS : (g + 1) * TILE_ROWS]


def local_mask(first_row, ends, keys, columns):
    column = lax.broadcasted_iota(jnp.int32, (1, columns), 1)
    row = first_row + lax.rem(column, TILE_ROWS)
    start = jnp.zeros((1, columns), jnp.int32)
    for end in ends:
        start = jnp.where(row >= end, end, start)
    key = lax.broadcasted_iota(jnp.int32, (keys, columns), 0)
    return (key >= start) & (key <= row)


def gather_kernel(*refs):
    scalars = refs[:5]
    query, grad, moved_out, early_out, late_out, counts_out = refs[5:]
    own, total, _ = plan(scalars)
    device, _, lengths, prompt_of, prompt_owner = scalars

    def add(response, sum_of_mine):
        mine = prompt_owner[prompt_of[response]] == device[0]
        return sum_of_mine + jnp.where(mine, lengths[response], 0)

    counts_out[0] = total - own
    counts_out[1] = lax.fori_loop(0, lengths.shape[0], add, jnp.int32(0)) - own
    rows = query.shape[0]
    half = rows // 2
    target = lax.broadcasted_iota(jnp.int32, (rows, rows), 0)
    source = lax.broadcasted_iota(jnp.int32, (rows, rows), 1)
    pick = ((source == target + own) & (source < total)).astype(BF16)
    for index, ref in enumerate((query, grad)):
        picked = dot(pick, ref[...]).astype(BF16)
        moved_out[index] = picked
        early_out[index] = picked[:half]
        late_out[index] = picked[half:]


def segment(
    count, offset, ends, query_tile, grad_tile, keys, values, local_keys, local_values,
    group, put, key_acc, value_acc, local_key_acc, local_value_acc,
):
    columns = group * TILE_ROWS
    keys_t = keys.T
    values_t = values.T
    local_keys_t = local_keys.T
    local_values_t = local_values.T
    scale2 = SCORE_SCALE * LOG2_E

    def body(tile, carry):
        row = pl.multiple_of(tile * TILE_ROWS, TILE_ROWS)
        within = row + lax.rem(lax.broadcasted_iota(jnp.int32, (columns, 1), 0), TILE_ROWS)
        query = jnp.where(within < count, query_tile(row), 0)
        grad = jnp.where(within < count, grad_tile(row), 0)
        query_t = query.T
        grad_t = grad.T
        within_t = row + lax.rem(lax.broadcasted_iota(jnp.int32, (1, columns), 1), TILE_ROWS)
        allowed = local_mask(row + offset, ends, local_keys.shape[0], columns)
        scores = dot(keys, query_t) * scale2
        local_scores = jnp.where(allowed, dot(local_keys, query_t) * scale2, NEGATIVE)
        top = jnp.maximum(
            jnp.max(scores, axis=0, keepdims=True), jnp.max(local_scores, axis=0, keepdims=True)
        )
        weight = jnp.exp2(scores - top)
        local_weight = jnp.exp2(local_scores - top)
        inverse = 1.0 / (
            jnp.sum(weight, axis=0, keepdims=True) + jnp.sum(local_weight, axis=0, keepdims=True)
        )
        weight = weight * inverse
        local_weight = local_weight * inverse
        weight_low = weight.astype(BF16)
        local_weight_low = local_weight.astype(BF16)
        out_t = dot(values_t, weight_low) + dot(local_values_t, local_weight_low)
        out_t = jnp.where(within_t < count, out_t, 0.0).astype(BF16)
        row_dot = jnp.sum(out_t.astype(F32) * grad_t.astype(F32), axis=0, keepdims=True)
        grad_scores = (weight * (dot(values, grad_t) - row_dot)).astype(BF16)
        local_grad_scores = (local_weight * (dot(local_values, grad_t) - row_dot)).astype(BF16)
        grad_query_t = (
            dot(keys_t, grad_scores) + dot(local_keys_t, local_grad_scores)
        ) * SCORE_SCALE
        if key_acc is not None:
            key_acc[...] += dot(grad_scores, query)
            value_acc[...] += dot(weight_low, grad)
        local_key_acc[...] += dot(local_grad_scores, query) * SCORE_SCALE
        local_value_acc[...] += dot(local_weight_low, grad)
        put(tile, row, out_t.T, grad_query_t.astype(BF16).T, top, inverse, row_dot)
        return carry

    lax.fori_loop(0, lax.div(count + TILE_ROWS - 1, TILE_ROWS), body, 0)


def own_kernel(*refs):
    scalars = refs[:5]
    query, grad, keys, values, local_keys, local_values = refs[5:11]
    out, grad_query, local_key, local_value, key_part, value_part = refs[11:]
    own, _, ends = plan(scalars)
    group = query.shape[1] // HEAD_WIDTH
    for ref in (out, grad_query, local_key, local_value, key_part, value_part):
        ref[...] = jnp.zeros(ref.shape, ref.dtype)

    def put(tile, row, out_tile, grad_query_tile, top, inverse, row_dot):
        put_tile(out, row, group, out_tile)
        put_tile(grad_query, row, group, grad_query_tile)

    segment(
        own, 0, ends,
        lambda row: tile_of(query, row, group), lambda row: tile_of(grad, row, group),
        keys[...], values[...], local_keys[...], local_values[...],
        group, put, key_part, value_part, local_key, local_value,
    )


def left_kernel(*refs):
    scalars = refs[:5]
    (rows, keys, values, local_keys, local_values,
     left_out, left_grad_query, key_acc, value_acc, stats) = refs[5:]
    own, total, ends = plan(scalars)
    count = total - own
    step = pl.program_id(0)
    heads = range(keys.shape[1] // HEAD_WIDTH)
    width = rows.shape[2] // len(heads)
    group = width // HEAD_WIDTH
    columns = group * TILE_ROWS
    all_rows = left_out.shape[0]
    for ref in (left_out, left_grad_query, key_acc, value_acc):
        ref[...] = jnp.zeros(ref.shape, ref.dtype)

    @pl.when(step == 0)
    def _():
        stats[...] = jnp.zeros(stats.shape, F32)

    scale2 = SCORE_SCALE * LOG2_E
    parts = chunks(keys.shape[0], KEY_CHUNK)

    def head_columns(head):
        return slice(head * HEAD_WIDTH, (head + 1) * HEAD_WIDTH)

    def body(tile, carry):
        row = pl.multiple_of(tile * TILE_ROWS, TILE_ROWS)
        queries = [tile_of(rows.at[0], row, group, head * width) for head in heads]
        grads = [tile_of(rows.at[1], row, group, head * width) for head in heads]
        within = row + lax.rem(lax.broadcasted_iota(jnp.int32, (columns, 1), 0), TILE_ROWS)
        place = within + own
        start = jnp.zeros((columns, 1), jnp.int32)
        for end in ends:
            start = jnp.where(place >= end, end, start)
        key = lax.broadcasted_iota(jnp.int32, (columns, all_rows), 1)
        allowed = (key >= start) & (key <= place)
        key_parts = [
            [keys[part, head_columns(head)] for part in parts] + [local_keys[:, head_columns(head)]]
            for head in heads
        ]
        value_parts = [
            [values[part, head_columns(head)] for part in parts] + [local_values[:, head_columns(head)]]
            for head in heads
        ]
        weights, tops, inverses = [], [], []
        for head in heads:
            scores = [dot_nt(queries[head], part) * scale2 for part in key_parts[head]]
            scores[-1] = jnp.where(allowed, scores[-1], NEGATIVE)
            top = functools.reduce(
                jnp.maximum, [jnp.max(score, axis=1, keepdims=True) for score in scores]
            )
            exponents = [jnp.exp2(score - top) for score in scores]
            inverse = 1.0 / sum(jnp.sum(part, axis=1, keepdims=True) for part in exponents)
            weights.append([part * inverse for part in exponents])
            tops.append(top)
            inverses.append(inverse)
        low = [[weight.astype(BF16) for weight in weights[head]] for head in heads]
        lane = lax.broadcasted_iota(jnp.int32, (columns, HEAD_WIDTH), 1)
        where = pl.ds(pl.multiple_of(tile * columns, columns), columns)
        for head in heads:
            result = sum(dot(weight, value) for weight, value in zip(low[head], value_parts[head]))
            result = jnp.where(within < count, result, 0.0).astype(BF16)
            row_dot = jnp.sum(
                result.astype(F32) * grads[head].astype(F32), axis=1, keepdims=True
            )
            grad_scores = [
                (weight * (dot_nt(grads[head], value) - row_dot)).astype(BF16)
                for weight, value in zip(weights[head], value_parts[head])
            ]
            grad_rows = sum(dot(score, part) for score, part in zip(grad_scores, key_parts[head]))
            put_tile(left_out, row, group, result, head * width)
            put_tile(left_grad_query, row, group, (grad_rows * SCORE_SCALE).astype(BF16), head * width)
            key_acc[:, head_columns(head)] += dot(grad_scores[-1].T, queries[head]) * SCORE_SCALE
            value_acc[:, head_columns(head)] += dot(low[head][-1].T, grads[head])
            packed = jnp.where(lane == 0, tops[head], jnp.where(lane == 1, inverses[head], row_dot)).T
            stats[pl.ds(pl.multiple_of((step * len(heads) + head) * 8, 8), 8), where] = packed[:8]
        return carry

    lax.fori_loop(0, lax.div(count + TILE_ROWS - 1, TILE_ROWS), body, 0)


def merge_kernel(*refs):
    scalars = refs[:5]
    owns, lefts, outs = refs[5:9], refs[9:13], refs[-4:]
    own, _, _ = plan(scalars)
    rows = outs[0].shape[0]
    target = lax.broadcasted_iota(jnp.int32, (rows, rows), 0)
    source = lax.broadcasted_iota(jnp.int32, (rows, rows), 1)
    place = (target == source + own).astype(BF16)
    for own_rows, left, out in zip(owns[:2], lefts[:2], outs[:2]):
        out[...] = (own_rows[...].astype(F32) + dot(place, left[...])).astype(BF16)
    for own_part, left, out in zip(owns[2:], lefts[2:], outs[2:]):
        out[...] = (own_part[...] + left[...]).astype(BF16)


def arrived_kernel(counts, first, second, stats, keys, values, own_key, own_value, *rest):
    key_out, value_out, key_acc, value_acc = rest[-4:]
    count = counts[1]
    heads = range(keys.shape[1] // HEAD_WIDTH)
    width = first.shape[2] // len(heads)
    group = width // HEAD_WIDTH
    columns = group * TILE_ROWS
    scale2 = SCORE_SCALE * LOG2_E
    key_acc[...] = own_key[...]
    value_acc[...] = own_value[...]
    parts = chunks(keys.shape[0], ARRIVED_CHUNK)
    tiles = lax.div(count + TILE_ROWS - 1, TILE_ROWS)
    full = first.shape[1] // TILE_ROWS

    def steps(rows, first_tile):
        def body(tile, carry):
            row = pl.multiple_of(tile * TILE_ROWS, TILE_ROWS)
            within = first_tile * TILE_ROWS + row + lax.rem(
                lax.broadcasted_iota(jnp.int32, (columns, 1), 0), TILE_ROWS
            )
            where = pl.ds(pl.multiple_of((first_tile + tile) * columns, columns), columns)
            queries, grads = [
                [tile_of(rows.at[index], row, group, head * width) for head in heads]
                for index in range(2)
            ]
            if first_tile:
                queries, grads = [
                    [jnp.where(within < count, tile, 0) for tile in tiles]
                    for tiles in (queries, grads)
                ]
            for part in parts:
                for head in heads:
                    here = slice(head * HEAD_WIDTH, (head + 1) * HEAD_WIDTH)
                    stat = stats[pl.ds(head * 8, 8), where]
                    weight = jnp.exp2(
                        dot_nt(keys[part, here], queries[head]) * scale2 - stat[0:1]
                    ) * stat[1:2]
                    grad_scores = (
                        weight * (dot_nt(values[part, here], grads[head]) - stat[2:3])
                    ).astype(BF16)
                    key_acc[part, here] += dot(grad_scores, queries[head])
                    value_acc[part, here] += dot(weight.astype(BF16), grads[head])
            return carry

        return body

    lax.fori_loop(0, jnp.minimum(tiles, full), steps(first, 0), 0)
    lax.fori_loop(0, jnp.maximum(tiles - full, 0), steps(second, full), 0)
    key_out[0] = (key_acc[...] * SCORE_SCALE).astype(BF16)
    value_out[0] = value_acc[...].astype(BF16)


def after(values, others):
    count = len(values)
    return pl.pallas_call(
        lambda *refs: None,
        in_specs=[pl.BlockSpec(memory_space=pl.ANY)] * (count + len(others)),
        out_specs=[pl.BlockSpec(memory_space=pl.ANY)] * count,
        out_shape=[jax.ShapeDtypeStruct(value.shape, value.dtype) for value in values],
        input_output_aliases={k: k for k in range(count)},
        name="after",
    )(*values, *others)


def send_late(late, send_count, receive_count, device):
    devices = lax.axis_size("dp")
    half = late.shape[1]
    if devices % 2:
        return shifted(late, "dp", -1)
    sizes = [size for size in (0, 8, 16, 32) if size < half] + [half]
    even = lax.rem(device, 2) == 0

    def branch(pairs, receives, size):
        def send(value, received):
            if size == 0:
                return received
            got = lax.ppermute(value[:, :size], "dp", pairs)
            got = jnp.pad(got, ((0, 0), (0, half - size), (0, 0)))
            return jnp.where(receives, got, received)

        return send

    received = late
    for parity in range(2):
        pairs = [(b, (b - 1) % devices) for b in range(parity, devices, 2)]
        sends = even == (parity == 0)
        count = jnp.where(sends, send_count, receive_count)
        choice = sum((count > half + size).astype(jnp.int32) for size in sizes[:-1])
        branches = [branch(pairs, jnp.logical_not(sends), size) for size in sizes]
        received = lax.switch(choice, branches, late, received)
    return received


def per_device(
    queries, response_key_rows, response_value_rows, shared_prompt_keys, shared_prompt_values,
    grad_out, lengths, packing, prompt_of, prompt_owner,
):
    rows = queries.shape[0]
    kv_heads = response_key_rows.shape[1] // HEAD_WIDTH
    width = queries.shape[1] // kv_heads
    prompt = shared_prompt_keys.shape[1]
    device = lax.axis_index("dp").astype(jnp.int32).reshape(1)
    scalars = (device, packing, lengths, prompt_of, prompt_owner)
    smem = [pl.BlockSpec(memory_space=pltpu.SMEM)] * 5
    params = pltpu.CompilerParams(vmem_limit_bytes=VMEM_LIMIT)
    cost = pl.CostEstimate(flops=1, bytes_accessed=1, transcendentals=0)
    shape = jax.ShapeDtypeStruct
    wide = pl.BlockSpec((rows, width), lambda h: (0, h))
    narrow = pl.BlockSpec((rows, HEAD_WIDTH), lambda h: (0, h))
    context = pl.BlockSpec((prompt, HEAD_WIDTH), lambda h: (0, h))
    pair = pl.BlockSpec((2, rows, width), lambda h: (0, 0, h))
    own_keys = shared_prompt_keys[0]
    own_values = shared_prompt_values[0]
    stat_columns = rows * width // HEAD_WIDTH

    left_keys = shifted(own_keys, "dp", 1)
    left_values = shifted(own_values, "dp", 1)

    half = rows // 2
    moved, early, late, counts = pl.pallas_call(
        gather_kernel,
        grid=(1,),
        in_specs=smem + [pl.BlockSpec(queries.shape, lambda i: (0, 0))] * 2,
        out_specs=[
            pl.BlockSpec((2, rows, queries.shape[1]), lambda i: (0, 0, 0)),
            pl.BlockSpec((2, half, queries.shape[1]), lambda i: (0, 0, 0)),
            pl.BlockSpec((2, half, queries.shape[1]), lambda i: (0, 0, 0)),
            pl.BlockSpec(memory_space=pltpu.SMEM),
        ],
        out_shape=[
            shape((2, rows, queries.shape[1]), BF16),
            shape((2, half, queries.shape[1]), BF16), shape((2, half, queries.shape[1]), BF16),
            shape((2,), jnp.int32),
        ],
        compiler_params=params,
        cost_estimate=cost,
        name="gather_rows",
    )(*scalars, queries, grad_out)

    own_out, own_grad_query, own_local_key, own_local_value, own_key, own_value = pl.pallas_call(
        own_kernel,
        grid=(kv_heads,),
        in_specs=smem + [wide, wide, context, context, narrow, narrow],
        out_specs=[wide, wide, narrow, narrow, context, context],
        out_shape=[
            shape(queries.shape, BF16), shape(queries.shape, BF16),
            shape(response_key_rows.shape, F32), shape(response_key_rows.shape, F32),
            shape(own_keys.shape, F32), shape(own_keys.shape, F32),
        ],
        compiler_params=params,
        cost_estimate=cost,
        name="own_rows",
    )(*scalars, queries, grad_out, own_keys, own_values, response_key_rows, response_value_rows)

    both = kv_heads // 2
    context_both = pl.BlockSpec((prompt, both * HEAD_WIDTH), lambda h: (0, h))

    wide_both = pl.BlockSpec((rows, both * width), lambda h: (0, h))
    narrow_both = pl.BlockSpec((rows, both * HEAD_WIDTH), lambda h: (0, h))
    pair_both = pl.BlockSpec((2, rows, both * width), lambda h: (0, 0, h))
    early, left_values = after((early, left_values), (left_keys, own_out))
    left_out, left_grad_query, left_local_key, left_local_value, stats = pl.pallas_call(
        left_kernel,
        grid=(2,),
        in_specs=smem + [pair_both, context_both, context_both, narrow_both, narrow_both],
        out_specs=[
            wide_both, wide_both, narrow_both, narrow_both,
            pl.BlockSpec((8 * kv_heads, stat_columns), lambda h: (0, 0)),
        ],
        out_shape=[
            shape(queries.shape, BF16), shape(queries.shape, BF16),
            shape(response_key_rows.shape, F32), shape(response_key_rows.shape, F32),
            shape((8 * kv_heads, stat_columns), F32),
        ],
        compiler_params=params,
        cost_estimate=cost,
        name="left_rows",
    )(*scalars, moved, left_keys, left_values, response_key_rows, response_value_rows)

    out, grad_query, local_key, local_value = pl.pallas_call(
        merge_kernel,
        grid=(kv_heads,),
        in_specs=smem + [wide, wide, narrow, narrow] * 2,
        out_specs=[wide, wide, narrow, narrow],
        out_shape=[
            shape(queries.shape, BF16), shape(queries.shape, BF16),
            shape(response_key_rows.shape, BF16), shape(response_key_rows.shape, BF16),
        ],
        compiler_params=params,
        cost_estimate=cost,
        name="merge_rows",
    )(*scalars, own_out, own_grad_query, own_local_key, own_local_value,
      left_out, left_grad_query, left_local_key, left_local_value)

    (late,) = after((late,), (out,))
    arrived_second = send_late(late, counts[0], counts[1], device[0])
    half_rows = pl.BlockSpec((2, half, both * width), lambda h: (0, 0, h))
    whole = pl.BlockSpec((1, prompt, both * HEAD_WIDTH), lambda h: (0, 0, h))
    prompt_key, prompt_value = pl.pallas_call(
        arrived_kernel,
        grid=(2,),
        in_specs=[
            pl.BlockSpec(memory_space=pltpu.SMEM), half_rows, half_rows,
            pl.BlockSpec((8 * both, stat_columns), lambda h: (h, 0)),
        ] + [context_both] * 4,
        out_specs=[whole, whole],
        out_shape=[shape((1,) + own_keys.shape, BF16)] * 2,
        scratch_shapes=[pltpu.VMEM((prompt, both * HEAD_WIDTH), F32)] * 2,
        compiler_params=params,
        cost_estimate=cost,
        name="arrived_rows",
    )(counts, shifted(early, "dp", -1), arrived_second, shifted(stats, "dp", -1),
      own_keys, own_values, own_key, own_value)
    return out, grad_query, local_key, local_value, prompt_key, prompt_value


def solution(mesh):
    rows = P(("groups", "dp"), "tensor")
    prompts = P(("groups", "dp"), None, "tensor")
    in_specs = (
        rows, rows, rows, prompts, prompts, rows,
        P("groups"), P(("groups", "dp"), None), P("groups"), P("groups"),
    )
    out_specs = (rows, rows, rows, rows, prompts, prompts)
    return jax.shard_map(
        per_device, mesh=mesh, in_specs=in_specs, out_specs=out_specs, check_vma=False
    )
```

profile of v0, /device:TPU:0, one launch (start us, length us, event | category | flops | bytes accessed | tf_op | source)
XLA Modules:
  0.0 75.3 jit_solution(13860881389138407924)
XLA Ops:
  0.6 3.0 %collective-permute-start.8 = (bf16[768,512]{1,0:T(8,128)(2,1)}, bf16[768,512]{1,0:T(8,128)(2,1)S(1)}, u32[]{:S(2)}, u32[]{:S(2)}) collective-permute-start(bf16[768,512]{1,0:T(8,128)(2,1)} %bitcast.5), channel_id=1, source_target_pairs={{0,2},{2,4},{4,6},{6,8},{8,10},{10,12},{12,14},{14,0},{1,3},{3,5},... | collective-permute-start | bytes 2359304 | tf_op jit(solution)/shard_map/ppermute | solution.py:25
  3.7 1.5 %collective-permute-start.9 = (bf16[768,512]{1,0:T(8,128)(2,1)}, bf16[768,512]{1,0:T(8,128)(2,1)S(1)}, u32[]{:S(2)}, u32[]{:S(2)}) collective-permute-start(bf16[768,512]{1,0:T(8,128)(2,1)} %bitcast.8), channel_id=1, source_target_pairs={{0,2},{2,4},{4,6},{6,8},{8,10},{10,12},{12,14},{14,0},{1,3},{3,5},... | collective-permute-start | bytes 2359304 | tf_op jit(solution)/shard_map/ppermute | solution.py:25
  5.2 4.3 %gather_rows.1 = (bf16[2,128,4096]{2,1,0:T(8,128)(2,1)}, bf16[2,64,4096]{2,1,0:T(8,128)(2,1)}, bf16[2,64,4096]{2,1,0:T(8,128)(2,1)S(1)}, s32[2]{0:T(128)}) custom-call(s32[1]{0:T(128)} %bitcast.refs_0_, s32[1,6]{1,0:T(1,128)} %refs_1_.7, s32[32]{0:T(128)} %refs_2_.7, s32[32]{0:T(128)} %refs_3_.7, s32[8]{0:T(128)} %refs_4_.7, bf16[128,4096]{1,0:T(8,128)(2,1)} %refs_5_.3, ...), custom_call_target="tpu_custom_call" | custom-call | flops 1 | bytes 1 | tf_op jit(solution)/shard_map/gather_rows/pallas_call | solution.py:394
  9.4 15.3 %own_rows.1 = (bf16[128,4096]{1,0:T(8,128)(2,1)}, bf16[128,4096]{1,0:T(8,128)(2,1)}, f32[128,512]{1,0:T(8,128)}, f32[128,512]{1,0:T(8,128)}, f32[768,512]{1,0:T(8,128)}, /*index=5*/f32[768,512]{1,0:T(8,128)}) custom-call(s32[1]{0:T(128)} %bitcast.refs_0_, s32[1,6]{1,0:T(1,128)} %refs_1_.7, s32[32]{0:T(128)} %refs_2_.7, s32[32]{0:T(128)} %refs_3_.7, ...), custom_call_target="tpu_custom_call" | custom-call | flops 1 | bytes 1 | tf_op jit(solution)/shard_map/own_rows/pallas_call | solution.py:414
  24.8 0.5 collective-permute-done.8.refs_2_.refs_6_
  25.3 0.0 copy-start
  25.3 16.0 %collective-permute-done.9.refs_1_ = bf16[768,512]{1,0:T(8,128)(2,1)S(1)} collective-permute-done((bf16[768,512]{1,0:T(8,128)(2,1)}, bf16[768,512]{1,0:T(8,128)(2,1)S(1)}, u32[]{:S(2)}, u32[]{:S(2)}) %collective-permute-start.9) | collective-permute-done | bytes 786464 | tf_op jit(solution)/shard_map/ppermute | solution.py:25
  41.3 0.0 copy-start.1
  41.3 0.0 copy-done
  41.3 0.9 %copy-done.1 = bf16[768,512]{1,0:T(8,128)(2,1)} copy-done((bf16[768,512]{1,0:T(8,128)(2,1)}, bf16[768,512]{1,0:T(8,128)(2,1)S(1)}, u32[]{:S(2)}) %copy-start.1) | copy-done | bytes 786456
  42.2 1.7 %collective-permute-start.10 = (bf16[2,64,4096]{2,1,0:T(8,128)(2,1)}, bf16[2,64,4096]{2,1,0:T(8,128)(2,1)}, u32[]{:S(2)}, u32[]{:S(2)}) collective-permute-start(bf16[2,64,4096]{2,1,0:T(8,128)(2,1)} %get-tuple-element.123), channel_id=1, source_target_pairs={{0,14},{2,0},{4,2},{6,4},{8,6},{10,8},{12,10},{14,12},{1,15},{3,1}... | collective-permute-start | bytes 3145736 | tf_op jit(solution)/shard_map/ppermute | solution.py:25
  43.9 0.0 copy-start.3
  43.9 9.4 %left_rows.1 = (bf16[128,4096]{1,0:T(8,128)(2,1)}, bf16[128,4096]{1,0:T(8,128)(2,1)}, f32[128,512]{1,0:T(8,128)}, f32[128,512]{1,0:T(8,128)}, f32[32,1024]{1,0:T(8,128)}) custom-call(s32[1]{0:T(128)} %bitcast.refs_0_, s32[1,6]{1,0:T(1,128)} %refs_1_.7, s32[32]{0:T(128)} %refs_2_.7, s32[32]{0:T(128)} %refs_3_.7, s32[8]{0:T(128)} %refs_4_.7, ...), custom_call_target="tpu_custom_call" | custom-call | flops 1 | bytes 1 | tf_op jit(solution)/shard_map/left_rows/pallas_call | solution.py:436
  53.4 1.4 %collective-permute-start.11 = (f32[32,1024]{1,0:T(8,128)}, f32[32,1024]{1,0:T(8,128)S(1)}, u32[]{:S(2)}, u32[]{:S(2)}) collective-permute-start(f32[32,1024]{1,0:T(8,128)} %get-tuple-element.125), channel_id=1, source_target_pairs={{0,14},{2,0},{4,2},{6,4},{8,6},{10,8},{12,10},{14,12},{1,15},{3,1}... | collective-permute-start | bytes 393224 | tf_op jit(solution)/shard_map/ppermute | solution.py:25
  54.8 0.0 copy-done.3
  54.8 0.6 fusion
  58.0 4.8 %merge_rows.1 = (bf16[128,4096]{1,0:T(8,128)(2,1)}, bf16[128,4096]{1,0:T(8,128)(2,1)}, bf16[128,512]{1,0:T(8,128)(2,1)}, bf16[128,512]{1,0:T(8,128)(2,1)}) custom-call(s32[1]{0:T(128)} %bitcast.refs_0_, s32[1,6]{1,0:T(1,128)} %refs_1_.7, s32[32]{0:T(128)} %refs_2_.7, s32[32]{0:T(128)} %refs_3_.7, s32[8]{0:T(128)} %refs_4_.7, ...), custom_call_target="tpu_custom_call" | custom-call | flops 1 | bytes 1 | tf_op jit(solution)/shard_map/merge_rows/pallas_call | solution.py:454
  62.8 0.1 conditional.2
  62.8 0.1 copy.22
  62.9 6.6 %collective-permute-done.11.stats = f32[32,1024]{1,0:T(8,128)S(1)} collective-permute-done((f32[32,1024]{1,0:T(8,128)}, f32[32,1024]{1,0:T(8,128)S(1)}, u32[]{:S(2)}, u32[]{:S(2)}) %collective-permute-start.11) | collective-permute-done | bytes 131104 | tf_op jit(solution)/shard_map/ppermute | solution.py:25
  69.5 0.0 copy-start.2
  69.5 0.0 collective-permute-done.10.first
  69.5 0.6 copy-done.2
  70.2 5.1 %arrived_rows.1 = (bf16[1,768,512]{2,1,0:T(8,128)(2,1)}, bf16[1,768,512]{2,1,0:T(8,128)(2,1)}) custom-call(s32[2]{0:T(128)} %get-tuple-element.122.counts, bf16[2,64,4096]{2,1,0:T(8,128)(2,1)} %collective-permute-done.10.first, bf16[2,64,4096]{2,1,0:T(8,128)(2,1)S(1)} %get-tuple-element.137.second, f32[32,1024]{1,0:T(8,128)} %copy-done.2, ...), custom_call_target="tpu_custom_call" | custom-call | flops 1 | bytes 1 | tf_op jit(solution)/shard_map/arrived_rows/pallas_call | solution.py:473
  (3 shorter events, 0.0 us)
Async XLA Ops:
  0.6 24.6 %collective-permute-start.8 = (bf16[768,512]{1,0:T(8,128)(2,1)}, bf16[768,512]{1,0:T(8,128)(2,1)S(1)}, u32[]{:S(2)}, u32[]{:S(2)}) collective-permute-start(bf16[768,512]{1,0:T(8,128)(2,1)} %bitcast.5), channel_id=1, source_target_pairs={{0,2},{2,4},{4,6},{6,8},{8,10},{10,12},{12,14},{14,0},{1,3},{3,5},... | collective-permute-start | bytes 2359304 | tf_op jit(solution)/shard_map/ppermute | solution.py:25
  3.7 37.6 %collective-permute-start.9 = (bf16[768,512]{1,0:T(8,128)(2,1)}, bf16[768,512]{1,0:T(8,128)(2,1)S(1)}, u32[]{:S(2)}, u32[]{:S(2)}) collective-permute-start(bf16[768,512]{1,0:T(8,128)(2,1)} %bitcast.8), channel_id=1, source_target_pairs={{0,2},{2,4},{4,6},{6,8},{8,10},{10,12},{12,14},{14,0},{1,3},{3,5},... | collective-permute-start | bytes 2359304 | tf_op jit(solution)/shard_map/ppermute | solution.py:25
  25.3 16.0 %copy-start = (bf16[768,512]{1,0:T(8,128)(2,1)}, bf16[768,512]{1,0:T(8,128)(2,1)S(1)}, u32[]{:S(2)}) copy-start(bf16[768,512]{1,0:T(8,128)(2,1)S(1)} %collective-permute-done.8.refs_2_.refs_6_) | copy-start | bytes 2359300
  41.3 0.9 %copy-start.1 = (bf16[768,512]{1,0:T(8,128)(2,1)}, bf16[768,512]{1,0:T(8,128)(2,1)S(1)}, u32[]{:S(2)}) copy-start(bf16[768,512]{1,0:T(8,128)(2,1)S(1)} %collective-permute-done.9.refs_1_) | copy-start | bytes 2359300
  42.2 27.4 %collective-permute-start.10 = (bf16[2,64,4096]{2,1,0:T(8,128)(2,1)}, bf16[2,64,4096]{2,1,0:T(8,128)(2,1)}, u32[]{:S(2)}, u32[]{:S(2)}) collective-permute-start(bf16[2,64,4096]{2,1,0:T(8,128)(2,1)} %get-tuple-element.123), channel_id=1, source_target_pairs={{0,14},{2,0},{4,2},{6,4},{8,6},{10,8},{12,10},{14,12},{1,15},{3,1}... | collective-permute-start | bytes 3145736 | tf_op jit(solution)/shard_map/ppermute | solution.py:25
  43.9 10.9 %copy-start.3 = (s32[2]{0:T(128)S(1)}, s32[2]{0:T(128)}, u32[]{:S(2)}) copy-start(s32[2]{0:T(128)} %get-tuple-element.122.counts) | copy-start | bytes 28
  53.4 16.2 %collective-permute-start.11 = (f32[32,1024]{1,0:T(8,128)}, f32[32,1024]{1,0:T(8,128)S(1)}, u32[]{:S(2)}, u32[]{:S(2)}) collective-permute-start(f32[32,1024]{1,0:T(8,128)} %get-tuple-element.125), channel_id=1, source_target_pairs={{0,14},{2,0},{4,2},{6,4},{8,6},{10,8},{12,10},{14,12},{1,15},{3,1}... | collective-permute-start | bytes 393224 | tf_op jit(solution)/shard_map/ppermute | solution.py:25
  69.5 0.7 copy-start.2
where the time goes:
time: 75.7 us; the launch traced here: 75.3 us
  Pallas kernels  38.9 us (51%)
  waiting for transfers between devices  23.1 us (31%)
  starting transfers between devices  7.72 us (10%)
  between operations  3.3 us (4%)
  local copies, waits for them, and re-layouts  2.19 us (3%)
    ppermute x4, waiting for transfers between devices, shifted(): return lax.ppermute(value, axis, pairs)  23.1 us
    pallas_call x1, Pallas kernels, per_device(): pl.pallas_call(own_kernel, grid=(kv_heads,), in_specs=smem + [wide, wide,...  15.3 us
    pallas_call x1, Pallas kernels, per_device(): pl.pallas_call(left_kernel, grid=(2,), in_specs=smem + [pair_both, contex...  9.44 us
    ppermute x4, starting transfers between devices, shifted(): return lax.ppermute(value, axis, pairs)  7.72 us
    pallas_call x1, Pallas kernels, per_device(): pl.pallas_call(arrived_kernel, grid=(2,), in_specs=[pl.BlockSpec(memory_s...  5.08 us
    pallas_call x1, Pallas kernels, per_device(): pl.pallas_call(merge_kernel, grid=(kv_heads,), in_specs=smem + [wide, wid...  4.77 us
    pallas_call x1, Pallas kernels, per_device(): pl.pallas_call(gather_kernel, grid=(1,), in_specs=smem + [pl.BlockSpec(qu...  4.27 us
    unnamed x8, local copies, waits for them, and re-layouts  1.53 us
  transfers between devices with their start and end apart: 4, of which 3 were waited for; matrix products, arithmetic and copies ran while one was open for 1% of the time, Pallas kernels for 45%

commit v1 on v0

--- a/solution.py
+++ b/solution.py
@@ -14,7 +14,7 @@
 NEGATIVE = -1e30
 F32 = jnp.float32
 BF16 = jnp.bfloat16
-VMEM_LIMIT = 60 * 1024 * 1024
+VMEM_LIMIT = 64 * 1024 * 1024
 KEY_CHUNK = 256
 ARRIVED_CHUNK = 768
 
@@ -183,18 +183,13 @@
      left_out, left_grad_query, key_acc, value_acc, stats) = refs[5:]
     own, total, ends = plan(scalars)
     count = total - own
-    step = pl.program_id(0)
     heads = range(keys.shape[1] // HEAD_WIDTH)
     width = rows.shape[2] // len(heads)
     group = width // HEAD_WIDTH
     columns = group * TILE_ROWS
     all_rows = left_out.shape[0]
-    for ref in (left_out, left_grad_query, key_acc, value_acc):
+    for ref in (left_out, left_grad_query, key_acc, value_acc, stats):
         ref[...] = jnp.zeros(ref.shape, ref.dtype)
-
-    @pl.when(step == 0)
-    def _():
-        stats[...] = jnp.zeros(stats.shape, F32)
 
     scale2 = SCORE_SCALE * LOG2_E
     parts = chunks(keys.shape[0], KEY_CHUNK)
@@ -252,7 +247,7 @@
             key_acc[:, head_columns(head)] += dot(grad_scores[-1].T, queries[head]) * SCORE_SCALE
             value_acc[:, head_columns(head)] += dot(low[head][-1].T, grads[head])
             packed = jnp.where(lane == 0, tops[head], jnp.where(lane == 1, inverses[head], row_dot)).T
-            stats[pl.ds(pl.multiple_of((step * len(heads) + head) * 8, 8), 8), where] = packed[:8]
+            stats[head * 4 : (head + 1) * 4, where] = packed[:4]
         return carry
 
     lax.fori_loop(0, lax.div(count + TILE_ROWS - 1, TILE_ROWS), body, 0)
@@ -305,7 +300,7 @@
             for part in parts:
                 for head in heads:
                     here = slice(head * HEAD_WIDTH, (head + 1) * HEAD_WIDTH)
-                    stat = stats[pl.ds(head * 8, 8), where]
+                    stat = stats[head * 4 : (head + 1) * 4, where]
                     weight = jnp.exp2(
                         dot_nt(keys[part, here], queries[head]) * scale2 - stat[0:1]
                     ) * stat[1:2]
@@ -439,12 +434,12 @@
         in_specs=smem + [pair_both, context_both, context_both, narrow_both, narrow_both],
         out_specs=[
             wide_both, wide_both, narrow_both, narrow_both,
-            pl.BlockSpec((8 * kv_heads, stat_columns), lambda h: (0, 0)),
+            pl.BlockSpec((4 * both, stat_columns), lambda h: (h, 0)),
         ],
         out_shape=[
             shape(queries.shape, BF16), shape(queries.shape, BF16),
             shape(response_key_rows.shape, F32), shape(response_key_rows.shape, F32),
-            shape((8 * kv_heads, stat_columns), F32),
+            shape((4 * kv_heads, stat_columns), F32),
         ],
         compiler_params=params,
         cost_estimate=cost,
@@ -475,7 +470,7 @@
         grid=(2,),
         in_specs=[
             pl.BlockSpec(memory_space=pltpu.SMEM), half_rows, half_rows,
-            pl.BlockSpec((8 * both, stat_columns), lambda h: (h, 0)),
+            pl.BlockSpec((4 * both, stat_columns), lambda h: (h, 0)),
         ] + [context_both] * 4,
         out_specs=[whole, whole],
         out_shape=[shape((1,) + own_keys.shape, BF16)] * 2,

time: 75.7 us -> 75.1 us (level)
  waiting for transfers between devices: 23.1 us -> 18.7 us
  Pallas kernels: 38.9 us -> 41.3 us
  local copies, waits for them, and re-layouts: 2.19 us -> 3.65 us
    ppermute x4, waiting for transfers between devices: 23.1 us -> 18.7 us  [shifted(): return lax.ppermute(value, axis, pairs)]
    cond x1, local copies, waits for them, and re-layouts: 0.07 us -> 2.31 us
    pallas_call x1, Pallas kernels: 5.08 us -> 7.25 us  [per_device(): pl.pallas_call(arrived_kernel, grid=(2,), in_specs=[pl.BlockSpec(memory_s...]
    unnamed x8 -> x0, local copies, waits for them, and re-layouts: 1.53 us -> none
  transfers between devices with their start and end apart: 4 -> 4, of which waited for: 3 -> 3; matrix products, arithmetic and copies ran while one was open for 1% -> 5% of each run, Pallas kernels for 45% -> 46%
where the time goes in v1:
time: 75.1 us; the launch traced here: 74.7 us
  Pallas kernels  41.3 us (55%)
  waiting for transfers between devices  18.7 us (25%)
  starting transfers between devices  7.73 us (10%)
  local copies, waits for them, and re-layouts  3.65 us (5%)
  between operations  3.28 us (4%)
    ppermute x4, waiting for transfers between devices, shifted(): return lax.ppermute(value, axis, pairs)  18.7 us
    pallas_call x1, Pallas kernels, per_device(): pl.pallas_call(own_kernel, grid=(kv_heads,), in_specs=smem + [wide, wide,...  15.3 us
    pallas_call x1, Pallas kernels, per_device(): pl.pallas_call(left_kernel, grid=(2,), in_specs=smem + [pair_both, contex...  9.39 us
    ppermute x4, starting transfers between devices, shifted(): return lax.ppermute(value, axis, pairs)  7.73 us
    pallas_call x1, Pallas kernels, per_device(): pl.pallas_call(arrived_kernel, grid=(2,), in_specs=[pl.BlockSpec(memory_s...  7.25 us
    pallas_call x1, Pallas kernels, per_device(): pl.pallas_call(merge_kernel, grid=(kv_heads,), in_specs=smem + [wide, wid...  4.74 us
    pallas_call x1, Pallas kernels, per_device(): pl.pallas_call(gather_kernel, grid=(1,), in_specs=smem + [pl.BlockSpec(qu...  4.64 us
    cond x1, local copies, waits for them, and re-layouts  2.31 us
  transfers between devices with their start and end apart: 4, of which 3 were waited for; matrix products, arithmetic and copies ran while one was open for 5% of the time, Pallas kernels for 46%

profile of v1, /device:TPU:0, one launch (start us, length us, event | category | flops | bytes accessed | tf_op | source)
XLA Modules:
  0.0 74.7 jit_solution(16149703888894226426)
XLA Ops:
  0.6 3.0 %collective-permute-start.8 = (bf16[768,512]{1,0:T(8,128)(2,1)}, bf16[768,512]{1,0:T(8,128)(2,1)}, u32[]{:S(2)}, u32[]{:S(2)}) collective-permute-start(bf16[768,512]{1,0:T(8,128)(2,1)} %bitcast.5), channel_id=1, source_target_pairs={{0,2},{2,4},{4,6},{6,8},{8,10},{10,12},{12,14},{14,0},{1,3},{3,5},... | collective-permute-start | bytes 2359304 | tf_op jit(solution)/shard_map/ppermute | solution.py:25
  3.7 1.5 %collective-permute-start.9 = (bf16[768,512]{1,0:T(8,128)(2,1)}, bf16[768,512]{1,0:T(8,128)(2,1)}, u32[]{:S(2)}, u32[]{:S(2)}) collective-permute-start(bf16[768,512]{1,0:T(8,128)(2,1)} %bitcast.8), channel_id=1, source_target_pairs={{0,2},{2,4},{4,6},{6,8},{8,10},{10,12},{12,14},{14,0},{1,3},{3,5},... | collective-permute-start | bytes 2359304 | tf_op jit(solution)/shard_map/ppermute | solution.py:25
  5.2 4.6 %gather_rows.1 = (bf16[2,128,4096]{2,1,0:T(8,128)(2,1)}, bf16[2,64,4096]{2,1,0:T(8,128)(2,1)}, bf16[2,64,4096]{2,1,0:T(8,128)(2,1)}, s32[2]{0:T(128)}) custom-call(s32[1]{0:T(128)} %bitcast.refs_0_, s32[1,6]{1,0:T(1,128)} %refs_1_.7, s32[32]{0:T(128)} %refs_2_.7, s32[32]{0:T(128)} %refs_3_.7, s32[8]{0:T(128)} %refs_4_.7, bf16[128,4096]{1,0:T(8,128)(2,1)} %refs_5_.3, ...), custom_call_target="tpu_custom_call" | custom-call | flops 1 | bytes 1 | tf_op jit(solution)/shard_map/gather_rows/pallas_call | solution.py:389
  9.8 15.3 %own_rows.1 = (bf16[128,4096]{1,0:T(8,128)(2,1)}, bf16[128,4096]{1,0:T(8,128)(2,1)}, f32[128,512]{1,0:T(8,128)}, f32[128,512]{1,0:T(8,128)}, f32[768,512]{1,0:T(8,128)}, /*index=5*/f32[768,512]{1,0:T(8,128)}) custom-call(s32[1]{0:T(128)} %bitcast.refs_0_, s32[1,6]{1,0:T(1,128)} %refs_1_.7, s32[32]{0:T(128)} %refs_2_.7, s32[32]{0:T(128)} %refs_3_.7, ...), custom_call_target="tpu_custom_call" | custom-call | flops 1 | bytes 1 | tf_op jit(solution)/shard_map/own_rows/pallas_call | solution.py:409
  25.1 0.3 collective-permute-done.8.refs_2_.refs_6_
  25.4 16.0 %collective-permute-done.9.refs_1_ = bf16[768,512]{1,0:T(8,128)(2,1)} collective-permute-done((bf16[768,512]{1,0:T(8,128)(2,1)}, bf16[768,512]{1,0:T(8,128)(2,1)}, u32[]{:S(2)}, u32[]{:S(2)}) %collective-permute-start.9) | collective-permute-done | bytes 786464 | tf_op jit(solution)/shard_map/ppermute | solution.py:25
  41.4 1.7 %collective-permute-start.10 = (bf16[2,64,4096]{2,1,0:T(8,128)(2,1)}, bf16[2,64,4096]{2,1,0:T(8,128)(2,1)}, u32[]{:S(2)}, u32[]{:S(2)}) collective-permute-start(bf16[2,64,4096]{2,1,0:T(8,128)(2,1)} %get-tuple-element.123), channel_id=1, source_target_pairs={{0,14},{2,0},{4,2},{6,4},{8,6},{10,8},{12,10},{14,12},{1,15},{3,1}... | collective-permute-start | bytes 3145736 | tf_op jit(solution)/shard_map/ppermute | solution.py:25
  43.1 9.4 %left_rows.1 = (bf16[128,4096]{1,0:T(8,128)(2,1)}, bf16[128,4096]{1,0:T(8,128)(2,1)}, f32[128,512]{1,0:T(8,128)}, f32[128,512]{1,0:T(8,128)}, f32[16,1024]{1,0:T(8,128)}) custom-call(s32[1]{0:T(128)} %bitcast.refs_0_, s32[1,6]{1,0:T(1,128)} %refs_1_.7, s32[32]{0:T(128)} %refs_2_.7, s32[32]{0:T(128)} %refs_3_.7, s32[8]{0:T(128)} %refs_4_.7, ...), custom_call_target="tpu_custom_call" | custom-call | flops 1 | bytes 1 | tf_op jit(solution)/shard_map/left_rows/pallas_call | solution.py:431
  52.5 1.5 %collective-permute-start.11 = (f32[16,1024]{1,0:T(8,128)}, f32[16,1024]{1,0:T(8,128)}, u32[]{:S(2)}, u32[]{:S(2)}) collective-permute-start(f32[16,1024]{1,0:T(8,128)} %get-tuple-element.125), channel_id=1, source_target_pairs={{0,14},{2,0},{4,2},{6,4},{8,6},{10,8},{12,10},{14,12},{1,15},{3,1}... | collective-permute-start | bytes 196616 | tf_op jit(solution)/shard_map/ppermute | solution.py:25
  54.0 1.3 %fusion = (s32[1]{0:T(128)}, s32[1]{0:T(128)}) fusion(s32[2]{0:T(128)} %get-tuple-element.122.counts), kind=kLoop, calls=%fused_computation.8 | loop fusion | bytes 16 | tf_op jit(solution)/shard_map/slice | solution.py:465
  57.9 4.7 %merge_rows.1 = (bf16[128,4096]{1,0:T(8,128)(2,1)}, bf16[128,4096]{1,0:T(8,128)(2,1)}, bf16[128,512]{1,0:T(8,128)(2,1)}, bf16[128,512]{1,0:T(8,128)(2,1)}) custom-call(s32[1]{0:T(128)} %bitcast.refs_0_, s32[1,6]{1,0:T(1,128)} %refs_1_.7, s32[32]{0:T(128)} %refs_2_.7, s32[32]{0:T(128)} %refs_3_.7, s32[8]{0:T(128)} %refs_4_.7, ...), custom_call_target="tpu_custom_call" | custom-call | flops 1 | bytes 1 | tf_op jit(solution)/shard_map/merge_rows/pallas_call | solution.py:449
  62.7 2.3 %conditional.2 = (bf16[2,64,4096]{2,1,0:T(8,128)(2,1)}) conditional(s32[]{:T(128)} %clamp.7, bf16[2,64,4096]{2,1,0:T(8,128)(2,1)} %after.3, (pred[]{:T(512)}, bf16[2,64,4096]{2,1,0:T(8,128)(2,1)}) %tuple.38, (pred[]{:T(512)}, bf16[2,64,4096]{2,1,0:T(8,128)(2,1)}) %tuple.38, (pred[]{:T(512)}, ...), branch_computations={%region_0.1_spmd, %region_1.2_spmd, %region_2.3_spmd, %region_3.4_... | conditional | flops 524289 | bytes 9961551 | solution.py:359
  62.7 2.3 %copy.22 = bf16[2,64,4096]{2,1,0:T(8,128)(2,1)} copy(bf16[2,64,4096]{2,1,0:T(8,128)(2,1)} %param) | data formatting | bytes 2097152 | tf_op jit(solution)/shard_map/cond
  65.0 2.4 %collective-permute-done.11.stats = f32[16,1024]{1,0:T(8,128)} collective-permute-done((f32[16,1024]{1,0:T(8,128)}, f32[16,1024]{1,0:T(8,128)}, u32[]{:S(2)}, u32[]{:S(2)}) %collective-permute-start.11) | collective-permute-done | bytes 65568 | tf_op jit(solution)/shard_map/ppermute | solution.py:25
  67.5 0.0 collective-permute-done.10.first
  67.5 7.2 %arrived_rows.1 = (bf16[1,768,512]{2,1,0:T(8,128)(2,1)}, bf16[1,768,512]{2,1,0:T(8,128)(2,1)}) custom-call(s32[2]{0:T(128)} %get-tuple-element.122.counts, bf16[2,64,4096]{2,1,0:T(8,128)(2,1)} %collective-permute-done.10.first, bf16[2,64,4096]{2,1,0:T(8,128)(2,1)} %get-tuple-element.137.second, f32[16,1024]{1,0:T(8,128)} %collective-permute-done.11.stats, ...), custom_call_target="tpu_custom_call" | custom-call | flops 1 | bytes 1 | tf_op jit(solution)/shard_map/arrived_rows/pallas_call | solution.py:468
  (3 shorter events, 0.0 us)
Async XLA Ops:
  0.6 24.7 %collective-permute-start.8 = (bf16[768,512]{1,0:T(8,128)(2,1)}, bf16[768,512]{1,0:T(8,128)(2,1)}, u32[]{:S(2)}, u32[]{:S(2)}) collective-permute-start(bf16[768,512]{1,0:T(8,128)(2,1)} %bitcast.5), channel_id=1, source_target_pairs={{0,2},{2,4},{4,6},{6,8},{8,10},{10,12},{12,14},{14,0},{1,3},{3,5},... | collective-permute-start | bytes 2359304 | tf_op jit(solution)/shard_map/ppermute | solution.py:25
  3.7 37.8 %collective-permute-start.9 = (bf16[768,512]{1,0:T(8,128)(2,1)}, bf16[768,512]{1,0:T(8,128)(2,1)}, u32[]{:S(2)}, u32[]{:S(2)}) collective-permute-start(bf16[768,512]{1,0:T(8,128)(2,1)} %bitcast.8), channel_id=1, source_target_pairs={{0,2},{2,4},{4,6},{6,8},{8,10},{10,12},{12,14},{14,0},{1,3},{3,5},... | collective-permute-start | bytes 2359304 | tf_op jit(solution)/shard_map/ppermute | solution.py:25
  41.4 26.1 %collective-permute-start.10 = (bf16[2,64,4096]{2,1,0:T(8,128)(2,1)}, bf16[2,64,4096]{2,1,0:T(8,128)(2,1)}, u32[]{:S(2)}, u32[]{:S(2)}) collective-permute-start(bf16[2,64,4096]{2,1,0:T(8,128)(2,1)} %get-tuple-element.123), channel_id=1, source_target_pairs={{0,14},{2,0},{4,2},{6,4},{8,6},{10,8},{12,10},{14,12},{1,15},{3,1}... | collective-permute-start | bytes 3145736 | tf_op jit(solution)/shard_map/ppermute | solution.py:25
  52.5 14.9 %collective-permute-start.11 = (f32[16,1024]{1,0:T(8,128)}, f32[16,1024]{1,0:T(8,128)}, u32[]{:S(2)}, u32[]{:S(2)}) collective-permute-start(f32[16,1024]{1,0:T(8,128)} %get-tuple-element.125), channel_id=1, source_target_pairs={{0,14},{2,0},{4,2},{6,4},{8,6},{10,8},{12,10},{14,12},{1,15},{3,1}... | collective-permute-start | bytes 196616 | tf_op jit(solution)/shard_map/ppermute | solution.py:25
